TPU v7x, 512 devices: a whole 4x4x16 slice. The times are simulated.
512 devices in a mesh: seq: 8 (over x, core), head: 64 (over y, z).
Axes of the slice: x: 4, y: 4, z: 16, core: 2. Of those that a mesh axis runs over, the one named last changes fastest.
Arguments:
- q_rot: bfloat16 [8192, 8192], P(('seq', 'head')), may hold values from -4 to 4
- k_rot: bfloat16 [8192, 1024], P(('seq', 'head')), may hold values from -7 to 7
- v_rot: bfloat16 [8192, 1024], P(('seq', 'head')), may hold values from -6 to 6
- q_exp: int32 [512, 256], P(('seq', 'head')), may hold values from 0 to 1
- k_exp: int32 [512, 32], P(('seq', 'head')), may hold values from 0 to 1
- v_exp: int32 [512, 32], P(('seq', 'head')), may hold values from -1 to 1
- span_order: int32 [16], replicated, may hold values from 0 to 15, each once
- ffn_row: int32 [8, 1024], P('seq'), may hold values from 0 to 1023, each once within a row
Outputs:
- routed: bfloat16 [8192, 8192], P(('seq', 'head'))
Inputs may be any that keep to these rules, and one draw needn't show every extreme that they name: `span_order`: each number of 0 to 15 once. Each row of ffn_row holds every number of 0 to 1023 once.
All inputs are finite; a program needn't handle non-finite values.
Results may differ from a plain program's by a relative error of at most 0.004.
Values may be sent and summed in bfloat16 or wider, within the bound.
No kernel may reach another device: no remote copies, remote signals or barrier semaphores. Data moves between devices by JAX's collectives and lax.ppermute only.
A program may use at most 64 MiB of HBM per device.

v0:
```python
import functools
import math

import jax
import jax.numpy as jnp
from jax import lax
from jax.sharding import PartitionSpec as P

HD = 128
HQ_DEV = 1
GROUP = 8
HBLK = 32
QBLK = 16
CH_GRP = 2


NEG = -1e30


def hadamard(size_n):
    idx = jnp.arange(size_n, dtype=jnp.int32)
    common_bits = idx[:, None] & idx[None, :]
    parity = jnp.zeros((size_n, size_n), jnp.int32)
    for bit_pos in range(size_n.bit_length() - 1):
        parity = parity + (common_bits >> bit_pos & 1)
    sign_table = 1.0 - 2.0 * (parity % 2).astype(jnp.float32)
    return sign_table / math.sqrt(size_n)


def dequantize(values_in, exponents):
    row_count, col_count = values_in.shape
    factor = jnp.exp2(exponents.astype(jnp.float32))
    shaped = values_in.astype(jnp.float32).reshape(row_count // QBLK, QBLK, col_count // HBLK, HBLK)
    return (shaped * factor[:, None, :, None]).reshape(row_count, col_count).astype(jnp.bfloat16)


def positions(row_ids, block_order, span_len):
    slot = row_ids // span_len
    slot_match = slot[:, None] == jnp.arange(block_order.shape[0], dtype=jnp.int32)[None, :]
    span_start = jnp.sum(jnp.where(slot_match, block_order[None, :], 0), axis=1)
    return span_start * span_len + row_ids % span_len


def tile_update(held, q_tile, q_pos, key_tile, value_tile, pos_tile, score_scale):
    peak_old, sum_old, weighted_old = held
    scores = (
        jnp.einsum("qhd,kd->hqk", q_tile, key_tile, preferred_element_type=jnp.float32)
        * score_scale
    )
    allowed = (pos_tile[None, :] <= q_pos[:, None])[None]
    scores = jnp.where(allowed, scores, NEG)
    peak_new = jnp.maximum(peak_old, jnp.max(scores, axis=2))
    weights = jnp.where(allowed, jnp.exp(scores - peak_new[:, :, None]), 0.0)
    factor = jnp.exp(peak_old - peak_new)
    sum_new = sum_old * factor + jnp.sum(weights, axis=2)
    added = jnp.einsum(
        "hqk,kd->hqd", weights.astype(jnp.bfloat16), value_tile, preferred_element_type=jnp.float32
    )
    return (peak_new, sum_new, weighted_old * factor[:, :, None] + added)


def attend(running, queries, query_pos, key_deq, value_deq, key_pos):
    key_count = key_deq.shape[0]
    key_width = math.gcd(key_count, 512)
    key_steps = key_count // key_width
    score_scale = 1.0 / math.sqrt(key_deq.shape[1])
    tiles = (
        key_deq.reshape(key_steps, key_width, -1),
        value_deq.reshape(key_steps, key_width, -1),
        key_pos.reshape(key_steps, key_width),
    )

    def one_tile(carried, tile):
        key_tile, value_tile, pos_tile = tile
        peaks, sums, outs = ([], [], [])
        q_state = tuple((item for item in carried))
        compute = functools.partial(
            tile_update,
            q_tile=queries,
            q_pos=query_pos,
            key_tile=key_tile,
            value_tile=value_tile,
            pos_tile=pos_tile,
            score_scale=score_scale,
        )
        updated = compute(q_state)
        peaks.append(updated[0])
        sums.append(updated[1])
        outs.append(updated[2])
        return (
            (jnp.concatenate(peaks, 1), jnp.concatenate(sums, 1), jnp.concatenate(outs, 1)),
            None,
        )

    result, ignored = lax.scan(one_tile, running, tiles)
    return result


def widen(heads_in, row_count):
    spread = GROUP // HQ_DEV
    shaped = heads_in.reshape(row_count, -1, HD)
    return jnp.repeat(shaped, spread, axis=1).reshape(row_count, -1)


def per_device(q_rot, k_rot, v_rot, q_exp, k_exp, v_exp, span_order, ffn_row):
    heads_n = lax.axis_size("head")
    seq_index = lax.axis_index("seq")
    tok_dev = q_rot.shape[0]
    tok_grp = tok_dev * heads_n
    span_len = tok_grp // CH_GRP
    query_deq = dequantize(q_rot, q_exp)
    key_deq = dequantize(k_rot, k_exp)
    value_deq = dequantize(v_rot, v_exp)
    query_pos = positions(
        seq_index * tok_grp + jnp.arange(tok_grp, dtype=jnp.int32), span_order, span_len
    )
    initial = (
        jnp.full((HQ_DEV, tok_grp), NEG, jnp.float32),
        jnp.zeros((HQ_DEV, tok_grp), jnp.float32),
        jnp.zeros((HQ_DEV, tok_grp, HD), jnp.float32),
    )
    head_q, head_k, head_v = (
        lax.all_to_all(query_deq, "head", split_axis=1, concat_axis=0, tiled=True),
        lax.all_to_all(widen(key_deq, tok_dev), "head", split_axis=1, concat_axis=0, tiled=True),
        lax.all_to_all(widen(value_deq, tok_dev), "head", split_axis=1, concat_axis=0, tiled=True),
    )
    q_heads = head_q.reshape(tok_grp, HQ_DEV, HD)
    piece_k = lax.all_gather(head_k, "seq", axis=0, tiled=True)
    piece_v = lax.all_gather(head_v, "seq", axis=0, tiled=True)
    key_pos = positions(jnp.arange(piece_k.shape[0], dtype=jnp.int32), span_order, span_len)
    final_state = attend(initial, q_heads, query_pos, piece_k, piece_v, key_pos)
    peak_end, weight_sum, weighted = final_state
    merged_out = weighted / weight_sum[:, :, None]
    turned = jnp.einsum(
        "hqbj,jk->qhbk",
        merged_out.reshape(HQ_DEV, tok_grp, HD // HBLK, HBLK),
        hadamard(HBLK),
        precision=lax.Precision.HIGHEST,
    )
    flat = turned.reshape(tok_grp, HQ_DEV * HD).astype(jnp.bfloat16)
    placed = jnp.zeros_like(flat).at[ffn_row[0]].set(flat)
    return lax.all_to_all(placed, "head", split_axis=0, concat_axis=1, tiled=True)


def solution(mesh):
    return jax.shard_map(
        per_device,
        mesh=mesh,
        in_specs=(
            P(("seq", "head"), None),
            P(("seq", "head"), None),
            P(("seq", "head"), None),
            P(("seq", "head"), None),
            P(("seq", "head"), None),
            P(("seq", "head"), None),
            P(),
            P("seq", None),
        ),
        out_specs=P(("seq", "head"), None),
        check_vma=False,
    )
```

profile of v0, /device:TPU:6, one launch (start us, length us, event | category | flops | bytes accessed | tf_op | source)
XLA Modules:
  0.0 219.1 jit_solution(3757769685313360391)
XLA Ops:
  6.6 0.7 exponential_bitcast_fusion
  7.4 0.8 copy_bitcast_fusion.2
  8.3 39.6 %all_to_all.73 = bf16[16,64,128]{2,0,1:T(8,128)(2,1)} all-to-all(bf16[16,64,128]{2,0,1:T(8,128)(2,1)S(1)} %bitcast.127), channel_id=1, replica_groups=mesh['seq'=8,'head'=64] {'head'}, dimensions={1} | all-to-all | bytes 524288 | tf_op jit(solution)/shard_map/all_to_all | solution.py:125
  48.0 0.7 exponential_bitcast_fusion.1
  48.8 0.8 copy_bitcast_fusion.3
  49.6 26.6 %all_to_all.74 = bf16[16,64,128]{2,0,1:T(8,128)(2,1)} all-to-all(bf16[16,64,128]{2,0,1:T(8,128)(2,1)S(1)} %bitcast.128), channel_id=1, replica_groups=mesh['seq'=8,'head'=64] {'head'}, dimensions={1} | all-to-all | bytes 524288 | tf_op jit(solution)/shard_map/all_to_all | solution.py:124
  76.4 0.8 copy_bitcast_fusion.1
  77.2 6.4 %all-to-all-start.1 = ((bf16[16,64,128]{2,0,1:T(8,128)(2,1)}), bf16[16,64,128]{2,0,1:T(8,128)(2,1)S(1)}, u32[]{:S(2)}, u32[]{:S(2)}) async-start(bf16[16,64,128]{2,0,1:T(8,128)(2,1)} %copy_bitcast_fusion.1), calls=%async_computation.1 | async-start | bytes 524288 | tf_op jit(solution)/shard_map/all_to_all | solution.py:123
  84.1 19.1 %all-to-all-done.1 = bf16[16,64,128]{2,0,1:T(8,128)(2,1)S(1)} async-done(((bf16[16,64,128]{2,0,1:T(8,128)(2,1)}), bf16[16,64,128]{2,0,1:T(8,128)(2,1)S(1)}, u32[]{:S(2)}, u32[]{:S(2)}) %all-to-all-start.1) | async-done | bytes 262176 | tf_op jit(solution)/shard_map/all_to_all | solution.py:123
  103.2 3.9 %all-gather.3.cloned.1.call-done = bf16[8192,128]{1,0:T(8,128)(2,1)} async-done(((bf16[1024,128]{1,0:T(8,128)(2,1)}), bf16[8192,128]{1,0:T(8,128)(2,1)}) %all-gather.3.cloned.1.call-update) | async-done | bytes 2097168 | tf_op jit(solution)/shard_map/all_gather | solution.py:128
  107.1 63.0 %while.15 = (s32[]{:T(128)}, f32[1,1024]{1,0:T(1,128)S(1)}, f32[1,1024]{1,0:T(1,128)S(1)}, f32[1,1024,128]{2,1,0:T(8,128)S(1)}, s32[16,512]{1,0:T(8,128)S(1)}, /...) while((s32[]{:T(128)}, f32[1,1024]{1,0:T(1,128)S(1)}, ...), condition=%wide.region_5.6_spmd.clone, body=%wide.region_2.5_spmd.clone.sunk | while | flops 277222400 | bytes 7953533 | solution.py:95
  107.1 1.4 fusion.82
  108.5 0.6 fusion.84
  109.2 1.8 fusion.86
  111.0 1.4 fusion.82
  112.5 0.6 fusion.84
  113.1 1.8 fusion.86
  115.0 1.4 fusion.82
  116.4 0.6 fusion.84
  117.0 1.8 fusion.86
  118.9 1.4 fusion.82
  120.3 0.6 fusion.84
  121.0 1.8 fusion.86
  122.9 1.4 fusion.82
  124.3 0.6 fusion.84
  124.9 1.8 fusion.86
  126.8 1.4 fusion.82
  128.2 0.6 fusion.84
  128.9 1.8 fusion.86
  130.7 1.4 fusion.82
  132.1 0.6 fusion.84
  132.8 1.8 fusion.86
  134.7 1.4 fusion.82
  136.1 0.6 fusion.84
  136.7 1.8 fusion.86
  138.6 1.4 fusion.82
  140.0 0.6 fusion.84
  140.7 1.8 fusion.86
  142.6 1.4 fusion.82
  144.0 0.6 fusion.84
  144.6 1.8 fusion.86
  146.5 1.4 fusion.82
  147.9 0.6 fusion.84
  148.6 1.8 fusion.86
  150.4 1.4 fusion.82
  151.8 0.6 fusion.84
  152.5 1.8 fusion.86
  154.4 1.4 fusion.82
  155.8 0.6 fusion.84
  156.4 1.8 fusion.86
  158.3 1.4 fusion.82
  159.7 0.6 fusion.84
  160.4 1.8 fusion.86
  162.2 1.4 fusion.82
  163.6 0.6 fusion.84
  164.3 1.8 fusion.86
  166.2 1.4 fusion.82
  167.6 0.6 fusion.84
  168.2 1.8 fusion.86
  170.1 0.2 copy.32
  170.4 0.6 convolution_convert_fusion
  171.1 3.2 %scatter_custom_fusion = bf16[1024,128]{1,0:T(8,128)(2,1)S(1)} fusion(s32[1024]{0:T(1024)S(1)} %bitcast.138, bf16[1024,128]{1,0:T(8,128)(2,1)S(1)} %copy.33, bf16[]{:T(256)} %constant.97.clone.1), kind=kCustom, calls=%fused_computation.42 | custom fusion | bytes 262146 | tf_op jit(solution)/shard_map/scatter | solution.py:141
  174.4 37.2 %all_to_all.75 = bf16[64,16,128]{2,1,0:T(8,128)(2,1)S(1)} all-to-all(bf16[64,16,128]{2,1,0:T(8,128)(2,1)S(1)} %bitcast.126), channel_id=1, replica_groups=mesh['seq'=8,'head'=64] {'head'}, dimensions={0} | all-to-all | bytes 524288 | tf_op jit(solution)/shard_map/all_to_all | solution.py:142
  211.5 0.7 copy_bitcast_fusion
  (100 shorter events, 2.0 us)
Async XLA Ops:
  6.5 69.7 %copy-start.3 = (s32[1,256]{1,0:T(1,128)S(1)}, s32[1,256]{1,0:T(1,128)}, u32[]{:S(2)}) copy-start(s32[1,256]{1,0:T(1,128)} %param.13) | copy-start | bytes 3076
  6.5 69.9 %copy-start = (bf16[16,8192]{1,0:T(8,128)(2,1)S(1)}, bf16[16,8192]{1,0:T(8,128)(2,1)}, u32[]{:S(2)}) copy-start(bf16[16,8192]{1,0:T(8,128)(2,1)} %param.10) | copy-start | bytes 786436
  6.5 77.1 %copy-start.2 = (s32[16]{0:T(128)S(1)}, s32[16]{0:T(128)}, u32[]{:S(2)}) copy-start(s32[16]{0:T(128)} %param.16) | copy-start | bytes 196
  6.5 77.5 %copy-start.1 = (s32[1,1024]{1,0:T(1,128)S(1)}, s32[1,1024]{1,0:T(1,128)}, u32[]{:S(2)}) copy-start(s32[1,1024]{1,0:T(1,128)} %param.17) | copy-start | bytes 12292
  6.5 96.7 %all-gather.5.cloned.1.call-start = ((), (), s32[]{:S(2)}) async-start(), calls=%async_computation.5 | async-start | bytes 2359296 | tf_op jit(solution)/shard_map/all_gather | solution.py:129
  47.9 59.2 %all-gather.3.cloned.1.call-start = ((), (), s32[]{:S(2)}) async-start(), calls=%async_computation.4 | async-start | bytes 2359296 | tf_op jit(solution)/shard_map/all_gather | solution.py:128
  77.2 26.0 %all-to-all-start.1 = ((bf16[16,64,128]{2,0,1:T(8,128)(2,1)}), bf16[16,64,128]{2,0,1:T(8,128)(2,1)S(1)}, u32[]{:S(2)}, u32[]{:S(2)}) async-start(bf16[16,64,128]{2,0,1:T(8,128)(2,1)} %copy_bitcast_fusion.1), calls=%async_computation.1 | async-start | bytes 524288 | tf_op jit(solution)/shard_map/all_to_all | solution.py:123
Sparse Core Ops, SparseCore 0:
  48.0 23.6 all-gather.4
  76.3 30.7 all-gather.2
where the time goes:
time: 221 us; the launch traced here: 219 us
  blocking collectives  103 us (47%)
  matrix products  51.8 us (23%)
  waiting for transfers between devices  23.1 us (10%)
  other arithmetic  14.6 us (7%)
  between operations  13.6 us (6%)
  starting transfers between devices  6.5 us (3%)
  local copies, waits for them, and re-layouts  5.08 us (2%)
    all_to_all x1, blocking collectives, per_device(): lax.all_to_all(widen(value_deq, tok_dev), 'head', split_axis=1, concat_ax...  39.6 us
    all_to_all x1, blocking collectives, per_device(): lax.all_to_all(placed, 'head', split_axis=0, concat_axis=1, tiled=True)  37.2 us
    dot_general x16, matrix products, tile_update(): jnp.einsum('hqk,kd->hqd', weights.astype(jnp.bfloat16), value_tile, prefe...  29.3 us
    all_to_all x1, blocking collectives, per_device(): lax.all_to_all(widen(key_deq, tok_dev), 'head', split_axis=1, concat_axis...  26.6 us
    dot_general x16, matrix products, tile_update(): jnp.einsum('qhd,kd->hqk', q_tile, key_tile, preferred_element_type=jnp.fl...  21.9 us
    all_to_all x1, waiting for transfers between devices, per_device(): lax.all_to_all(query_deq, 'head', split_axis=1, concat_axis=0, tiled=True)  19.1 us
    reduce_sum x16, other arithmetic, tile_update(): sum_new = sum_old * factor + jnp.sum(weights, axis=2)  9.95 us
    all_to_all x1, starting transfers between devices, per_device(): lax.all_to_all(query_deq, 'head', split_axis=1, concat_axis=0, tiled=True)  6.42 us
  transfers between devices with their start and end apart: 3, of which 2 were waited for; matrix products, arithmetic and copies ran while one was open for 1% of the time, Pallas kernels for 0%

commit v1 on v0

v1 whole, which is shorter than its diff:
```python
import functools
import math

import jax
import jax.numpy as jnp
from jax import lax
from jax.experimental import pallas as pl
from jax.experimental.pallas import tpu as pltpu
from jax.sharding import PartitionSpec as P

HD = 128
GROUP = 8
HBLK = 32
QBLK = 16
TILES = 4

NEG = -1e30
NT = (((1,), (1,)), ((), ()))
TN = (((0,), (0,)), ((), ()))


def dequantize(values_in, exponents):
    row_count, col_count = values_in.shape
    factor = jnp.exp2(exponents.astype(jnp.float32))
    shaped = values_in.astype(jnp.float32).reshape(row_count // QBLK, QBLK, col_count // HBLK, HBLK)
    return (shaped * factor[:, None, :, None]).reshape(row_count, col_count).astype(jnp.bfloat16)


def folded(tile):
    return jnp.sum(tile.reshape(tile.shape[0] // 8, 8, tile.shape[1]), axis=0)


def sign_table():
    i = lax.broadcasted_iota(jnp.int32, (HD, HD), 0)
    j = lax.broadcasted_iota(jnp.int32, (HD, HD), 1)
    both = i & j
    odd = (both ^ (both >> 1) ^ (both >> 2) ^ (both >> 3) ^ (both >> 4)) & 1
    return jnp.where(i // HBLK == j // HBLK, 1.0 - 2.0 * odd.astype(jnp.float32), 0.0).astype(jnp.bfloat16)


def attend_kernel(order_ref, group_ref, q_ref, k_ref, v_ref, row_ref, o_ref, slot_ref, peak, total, acc, flat, *, span):
    spans = order_ref.shape[0]
    rows = q_ref.shape[0]
    q_spans = rows // span
    rate = math.log2(math.e) / math.sqrt(HD)

    def note(stored, _):
        slot_ref[order_ref[stored]] = stored
        return 0

    lax.fori_loop(0, spans, note, 0)

    def span_of(ref, slot):
        return ref[pl.ds(pl.multiple_of(slot * span, span), span), :]

    for a in range(q_spans):
        q = q_ref[pl.ds(a * span, span), :]
        own = group_ref[0] * q_spans + a
        count = order_ref[own]

        def scores(slot):
            return lax.dot_general(span_of(k_ref, slot), q, NT, preferred_element_type=jnp.float32)

        def mixed(slot, weights):
            return lax.dot_general(
                span_of(v_ref, slot), weights.astype(jnp.bfloat16), TN, preferred_element_type=jnp.float32
            )

        key_at = lax.broadcasted_iota(jnp.int32, (span, span), 0)
        query_at = lax.broadcasted_iota(jnp.int32, (span, span), 1)
        first = jnp.where(key_at <= query_at, scores(own), NEG)
        top = jnp.max(first, axis=0, keepdims=True)
        weights = jnp.exp2((first - top) * rate)
        peak[...] = top
        total[...] = folded(weights)
        acc[...] = mixed(own, weights)

        def earlier(slots):
            tiles = [scores(slot) for slot in slots]
            old = peak[...]
            top = old
            for tile in tiles:
                top = jnp.maximum(top, jnp.max(tile, axis=0, keepdims=True))
            shrink = jnp.exp2((old - top) * rate)
            peak[...] = top
            summed = total[...] * shrink
            added = acc[...] * shrink
            for slot, tile in zip(slots, tiles):
                weights = jnp.exp2((tile - top) * rate)
                summed = summed + folded(weights)
                added = added + mixed(slot, weights)
            total[...] = summed
            acc[...] = added

        def step(t, _):
            earlier([slot_ref[TILES * t + i] for i in range(TILES)])
            return 0

        lax.fori_loop(0, count // TILES, step, 0)
        part = TILES // 2
        while part:
            @pl.when((count & part) != 0)
            def _(part=part):
                base = count & ~(2 * part - 1)
                earlier([slot_ref[base + i] for i in range(part)])

            part //= 2

        out = acc[...] * (1.0 / (jnp.sum(total[...], axis=0, keepdims=True) * math.sqrt(HBLK)))
        high = out.astype(jnp.bfloat16)
        low = (out - high.astype(jnp.float32)).astype(jnp.bfloat16)
        signs = sign_table()
        turned = jnp.dot(signs, high, preferred_element_type=jnp.float32)
        turned = turned + jnp.dot(signs, low, preferred_element_type=jnp.float32)
        flat[:, pl.ds(a * span, span)] = turned.astype(jnp.bfloat16)

    block = math.gcd(rows, 256)
    for start in range(0, rows, block):
        want = lax.broadcasted_iota(jnp.int32, (block, rows), 0) + start
        pick = jnp.where(row_ref[...] == want, 1.0, 0.0).astype(jnp.bfloat16)
        o_ref[pl.ds(start, block), :] = lax.dot_general(
            pick, flat[...], NT, preferred_element_type=jnp.float32
        ).astype(jnp.bfloat16)


def attend(order, group, q, k, v, row):
    rows = q.shape[0]
    span = k.shape[0] // order.shape[0]
    vmem = pl.BlockSpec(memory_space=pltpu.VMEM)
    smem = pl.BlockSpec(memory_space=pltpu.SMEM)
    return pl.pallas_call(
        functools.partial(attend_kernel, span=span),
        out_shape=jax.ShapeDtypeStruct((rows, HD), jnp.bfloat16),
        in_specs=[smem, smem, vmem, vmem, vmem, vmem],
        out_specs=vmem,
        scratch_shapes=[
            pltpu.SMEM((order.shape[0],), jnp.int32),
            pltpu.VMEM((1, span), jnp.float32),
            pltpu.VMEM((8, span), jnp.float32),
            pltpu.VMEM((HD, span), jnp.float32),
            pltpu.VMEM((HD, rows), jnp.bfloat16),
        ],
        compiler_params=pltpu.CompilerParams(vmem_limit_bytes=40 * 2**20),
        name="attend",
    )(order, group, q, k, v, row)


def widen(heads_in, row_count):
    shaped = heads_in.reshape(row_count, -1, HD)
    return jnp.repeat(shaped, GROUP, axis=1).reshape(row_count, -1)


def per_device(q_rot, k_rot, v_rot, q_exp, k_exp, v_exp, span_order, ffn_row):
    tok_dev = q_rot.shape[0]
    group = lax.axis_index("seq").astype(jnp.int32).reshape(1)
    query_deq = dequantize(q_rot, q_exp)
    key_deq = dequantize(k_rot, k_exp)
    value_deq = dequantize(v_rot, v_exp)
    head_q, head_k, head_v = (
        lax.all_to_all(query_deq, "head", split_axis=1, concat_axis=0, tiled=True),
        lax.all_to_all(widen(key_deq, tok_dev), "head", split_axis=1, concat_axis=0, tiled=True),
        lax.all_to_all(widen(value_deq, tok_dev), "head", split_axis=1, concat_axis=0, tiled=True),
    )
    piece_k = lax.all_gather(head_k, "seq", axis=0, tiled=True)
    piece_v = lax.all_gather(head_v, "seq", axis=0, tiled=True)
    placed = attend(span_order, group, head_q, piece_k, piece_v, ffn_row)
    return lax.all_to_all(placed, "head", split_axis=0, concat_axis=1, tiled=True)


def solution(mesh):
    return jax.shard_map(
        per_device,
        mesh=mesh,
        in_specs=(
            P(("seq", "head"), None),
            P(("seq", "head"), None),
            P(("seq", "head"), None),
            P(("seq", "head"), None),
            P(("seq", "head"), None),
            P(("seq", "head"), None),
            P(),
            P("seq", None),
        ),
        out_specs=P(("seq", "head"), None),
        check_vma=False,
    )
```

time: 221 us -> 169 us (0.76)
  the two profiles are of different devices: /device:TPU:6 before, /device:TPU:4 now
where the time goes in v1:
time: 169 us
  blocking collectives  103 us (61%)
  waiting for transfers between devices  23.9 us (14%)
  between operations  13.5 us (8%)
  Pallas kernels  13.2 us (8%)
  starting transfers between devices  6.5 us (4%)
  local copies, waits for them, and re-layouts  4.46 us (3%)
  other arithmetic  3.68 us (2%)
    all_to_all x1, blocking collectives, per_device(): lax.all_to_all(widen(key_deq, tok_dev), 'head', split_axis=1, concat_axis...  39.6 us
    all_to_all x1, blocking collectives, per_device(): lax.all_to_all(placed, 'head', split_axis=0, concat_axis=1, tiled=True)  37.2 us
    all_to_all x1, blocking collectives, per_device(): lax.all_to_all(widen(value_deq, tok_dev), 'head', split_axis=1, concat_ax...  26.6 us
    all_to_all x1, waiting for transfers between devices, per_device(): lax.all_to_all(query_deq, 'head', split_axis=1, concat_axis=0, tiled=True)  19.6 us
    pallas_call x1, Pallas kernels, attend(): pl.pallas_call(functools.partial(attend_kernel, span=span), out_shape=jax...  13.2 us
    all_to_all x1, starting transfers between devices, per_device(): lax.all_to_all(query_deq, 'head', split_axis=1, concat_axis=0, tiled=True)  6.42 us
    all_gather x1, waiting for transfers between devices, per_device(): piece_v = lax.all_gather(head_v, 'seq', axis=0, tiled=True)  4.25 us
  transfers between devices with their start and end apart: 3, of which 2 were waited for; matrix products, arithmetic and copies ran while one was open for 2% of the time, Pallas kernels for 0%

profile of v1, /device:TPU:4, one launch (start us, length us, event | category | flops | bytes accessed | tf_op | source)
XLA Modules:
  0.0 168.6 jit_solution(12447039429733958619)
XLA Ops:
  6.5 0.0 copy-start.5
  6.5 0.0 copy-start.4
  6.5 0.0 copy-start.3
  6.5 0.0 copy-start.2
  6.5 0.0 all-gather.3.cloned.1.call-start
  6.6 0.7 exponential_bitcast_fusion.1
  7.3 0.1 mul.57
  7.4 0.1 mul.58
  7.4 0.8 copy_bitcast_fusion.3
  8.3 39.6 %all_to_all.76 = bf16[16,64,128]{2,0,1:T(8,128)(2,1)} all-to-all(bf16[16,64,128]{2,0,1:T(8,128)(2,1)S(1)} %bitcast.43), channel_id=1, replica_groups=mesh['seq'=8,'head'=64] {'head'}, dimensions={1} | all-to-all | bytes 524288 | tf_op jit(solution)/shard_map/all_to_all | solution.py:161
  47.9 0.0 all-gather.3.cloned.1.call-update
  47.9 0.0 all-gather.5.cloned.1.call-start
  48.0 0.7 exponential_bitcast_fusion
  48.6 0.1 mul.62
  48.7 0.1 mul.63
  48.8 0.8 copy_bitcast_fusion.2
  49.6 26.6 %all_to_all.77 = bf16[16,64,128]{2,0,1:T(8,128)(2,1)} all-to-all(bf16[16,64,128]{2,0,1:T(8,128)(2,1)S(1)} %bitcast.44), channel_id=1, replica_groups=mesh['seq'=8,'head'=64] {'head'}, dimensions={1} | all-to-all | bytes 524288 | tf_op jit(solution)/shard_map/all_to_all | solution.py:162
  76.2 0.0 all-gather.5.cloned.1.call-update
  76.2 0.0 copy-done.5
  76.2 0.1 mul.52
  76.3 0.1 mul.53
  76.4 0.0 copy-done.4
  76.4 0.8 copy_bitcast_fusion.1
  77.2 6.4 %all-to-all-start = ((bf16[16,64,128]{2,0,1:T(8,128)(2,1)}), bf16[16,64,128]{2,0,1:T(8,128)(2,1)S(1)}, u32[]{:S(2)}, u32[]{:S(2)}) async-start(bf16[16,64,128]{2,0,1:T(8,128)(2,1)} %copy_bitcast_fusion.1), calls=%async_computation | async-start | bytes 524288 | tf_op jit(solution)/shard_map/all_to_all | solution.py:160
  83.6 19.6 %all-to-all-done = bf16[16,64,128]{2,0,1:T(8,128)(2,1)S(1)} async-done(((bf16[16,64,128]{2,0,1:T(8,128)(2,1)}), bf16[16,64,128]{2,0,1:T(8,128)(2,1)S(1)}, u32[]{:S(2)}, u32[]{:S(2)}) %all-to-all-start) | async-done | bytes 262176 | tf_op jit(solution)/shard_map/all_to_all | solution.py:160
  103.2 0.0 all-gather.3.cloned.1.call-done.k_ref
  103.2 4.2 %all-gather.5.cloned.1.call-done.v_ref = bf16[8192,128]{1,0:T(8,128)(2,1)} async-done(((bf16[1024,128]{1,0:T(8,128)(2,1)}), bf16[8192,128]{1,0:T(8,128)(2,1)}) %all-gather.5.cloned.1.call-update) | async-done | bytes 2097168 | tf_op jit(solution)/shard_map/all_gather | solution.py:165
  107.5 0.0 copy-done.3
  107.5 0.0 copy-done.2
  107.5 0.0 copy-start
  107.5 1.6 copy-done
  109.1 0.0 copy-start.1
  109.1 1.6 copy-done.1
  110.6 13.2 %attend.1 = bf16[1024,128]{1,0:T(8,128)(2,1)S(1)} custom-call(s32[16]{0:T(128)S(1)} %copy-done.3, s32[1]{0:T(128)} %bitcast.group_ref, bf16[1024,128]{1,0:T(8,128)(2,1)S(1)} %bitcast.39, bf16[8192,128]{1,0:T(8,128)(2,1)S(1)} %copy-done, bf16[8192,128]{1,0:T(8,128)(2,1)S(1)} %copy-done.1, s32[1,1024]{1,0:T(1,128)S(1)} %copy-done.2), custom_call_target="tpu_custom_call" | custom-call | tf_op jit(solution)/shard_map/attend/pallas_call | solution.py:131
  123.8 37.2 %all_to_all.78 = bf16[64,16,128]{2,1,0:T(8,128)(2,1)S(1)} all-to-all(bf16[64,16,128]{2,1,0:T(8,128)(2,1)S(1)} %bitcast.40), channel_id=1, replica_groups=mesh['seq'=8,'head'=64] {'head'}, dimensions={0} | all-to-all | bytes 524288 | tf_op jit(solution)/shard_map/all_to_all | solution.py:167
  161.0 0.7 copy_bitcast_fusion
  (3 shorter events, 0.1 us)
Async XLA Ops:
  6.5 69.7 %copy-start.5 = (s32[1,256]{1,0:T(1,128)S(1)}, s32[1,256]{1,0:T(1,128)}, u32[]{:S(2)}) copy-start(s32[1,256]{1,0:T(1,128)} %param.11) | copy-start | bytes 3076
  6.5 69.9 %copy-start.4 = (bf16[16,8192]{1,0:T(8,128)(2,1)S(1)}, bf16[16,8192]{1,0:T(8,128)(2,1)}, u32[]{:S(2)}) copy-start(bf16[16,8192]{1,0:T(8,128)(2,1)} %param.8) | copy-start | bytes 786436
  6.5 100.9 %copy-start.3 = (s32[16]{0:T(128)S(1)}, s32[16]{0:T(128)}, u32[]{:S(2)}) copy-start(s32[16]{0:T(128)} %order_ref.1) | copy-start | bytes 196
  6.5 100.9 %copy-start.2 = (s32[1,1024]{1,0:T(1,128)S(1)}, s32[1,1024]{1,0:T(1,128)}, u32[]{:S(2)}) copy-start(s32[1,1024]{1,0:T(1,128)} %row_ref.1) | copy-start | bytes 12292
  6.5 96.7 %all-gather.3.cloned.1.call-start = ((), (), s32[]{:S(2)}) async-start(), calls=%async_computation.4 | async-start | bytes 2359296 | tf_op jit(solution)/shard_map/all_gather | solution.py:164
  47.9 59.6 %all-gather.5.cloned.1.call-start = ((), (), s32[]{:S(2)}) async-start(), calls=%async_computation.5 | async-start | bytes 2359296 | tf_op jit(solution)/shard_map/all_gather | solution.py:165
  77.2 26.0 %all-to-all-start = ((bf16[16,64,128]{2,0,1:T(8,128)(2,1)}), bf16[16,64,128]{2,0,1:T(8,128)(2,1)S(1)}, u32[]{:S(2)}, u32[]{:S(2)}) async-start(bf16[16,64,128]{2,0,1:T(8,128)(2,1)} %copy_bitcast_fusion.1), calls=%async_computation | async-start | bytes 524288 | tf_op jit(solution)/shard_map/all_to_all | solution.py:160
  107.5 1.6 copy-start
  109.1 1.6 copy-start.1
Sparse Core Ops, SparseCore 0:
  48.0 23.9 all-gather.2
  76.3 31.1 all-gather.4
